TPU v7x, 512 devices: a whole 4x8x8 slice. The times are simulated.
512 devices in a mesh: cuts: 8 (over x, core), rows: 64 (over z, y).
Axes of the slice: x: 4, y: 8, z: 8, core: 2. Of those that a mesh axis runs over, the one named last changes fastest.
Arguments:
- start_modes: float32 [8, 256, 512, 128], P('cuts', 'rows'), may hold values from -6 to 6
- contrast: float32 [8, 256, 512], P('cuts', 'rows'), may hold values from 0 to 1
- rotations: float32 [8, 2, 128, 128], P('cuts'), may hold values from -0.2 to 1.2, as said below
- ordering: int32 [8, 2, 128], P('cuts'), may hold values from 0 to 127, each once within a row
Outputs:
- modes: float32 [8, 256, 512, 128], P('cuts', 'rows')
- coupling: float32 [8, 128, 128], P('cuts', 'rows')
- rayleigh: float32 [8, 128, 128], P('cuts', 'rows')
Inputs may be any that keep to these rules, and one draw needn't show every extreme that they name: `rotations`: each matrix is invertible.
All inputs are finite; a program needn't handle non-finite values.
Results may differ from a plain program's by a relative error of at most 0.00026.
Values sent between devices are 32-bit elements; how exact they have to be, the bound alone decides.
A program may use at most 64 MiB of HBM per device.

v0:
```python
import jax
import jax.numpy as jnp
from jax import lax
from jax.sharding import PartitionSpec as P

DEGREE = 4
ITERS = 2


def padded_2(block, sides, width):
    for axis, dim in sides:
        count = lax.axis_size(axis)
        forward = [(i, i + 1) for i in range(count - 1)]
        backward = [(target, source) for source, target in forward]
        low = lax.ppermute(
            lax.slice_in_dim(block, block.shape[dim] - width, None, axis=dim), axis, forward
        )
        high = lax.ppermute(lax.slice_in_dim(block, 0, width, axis=dim), axis, backward)
        block = jnp.concatenate([low, block, high], axis=dim)
    return block


def from_behind(value, axis, by):
    peers = lax.axis_size(axis)
    pairs = [(i, i + by) for i in range(peers) if 0 <= i + by < peers]
    return lax.ppermute(value, axis, pairs)


def neighbour_sum(center, rows_source):
    columns = jnp.pad(center, ((0, 0), (1, 1), (0, 0)))
    return rows_source[2:] + rows_source[:-2] + columns[:, 2:] + columns[:, :-2]


def operator_core(center, rows_source, section):
    return (
        0.8 * (section[:, :, None] * center + 0.25 * neighbour_sum(center, rows_source))
        - 0.2 * center
    )


def inner_modes(left, right):
    return jnp.einsum("rcm,rcn->mn", left, right, precision=lax.Precision.HIGHEST)


def apply_edge(vectors, section):
    padded = padded_2(vectors, (("rows", 0),), 1)
    return operator_core(vectors, padded, section)


def body(start_modes, contrast, rotations, ordering):
    subspace = start_modes[0]
    section = contrast[0]
    turnings = rotations[0]
    sequence = ordering[0]
    rows_here = subspace.shape[0]
    columns = subspace.shape[1]
    nmodes = subspace.shape[2]
    tiles = lax.axis_size("rows")
    pixels = rows_here * tiles * columns
    for sweep in range(ITERS):
        before = subspace
        current = apply_edge(before, section)
        for degree_step in range(2, DEGREE + 1):
            following = 2.0 * apply_edge(current, section) - before
            before, current = (current, following)
        gram_sum = lax.psum(inner_modes(current, current), "rows") / pixels
        factor_low = jnp.linalg.cholesky(gram_sum)
        mixing = lax.linalg.triangular_solve(
            factor_low, turnings[sweep], left_side=True, lower=True, transpose_a=True
        )
        picker = (sequence[sweep][None, :] == jnp.arange(nmodes, dtype=jnp.int32)[:, None]).astype(
            jnp.float32
        )
        mixing = jnp.dot(mixing, picker, precision=lax.Precision.HIGHEST)
        subspace = jnp.einsum("rcm,mn->rcn", current, mixing, precision=lax.Precision.HIGHEST)
    earlier = from_behind(subspace, "cuts", 1)
    earlier = jnp.where(lax.axis_index("cuts") == 0, start_modes[0], earlier)
    applied = apply_edge(subspace, section)
    coupling_term = inner_modes(earlier, subspace)
    rayleigh_term = inner_modes(subspace, applied)
    share_rows = nmodes // tiles
    coupling_sum, rayleigh_sum = lax.psum((coupling_term, rayleigh_term), "rows")
    coupling_part = lax.dynamic_slice_in_dim(
        coupling_sum, lax.axis_index("rows") * share_rows, share_rows, 0
    )
    rayleigh_part = lax.dynamic_slice_in_dim(
        rayleigh_sum, lax.axis_index("rows") * share_rows, share_rows, 0
    )
    return (subspace[None], (coupling_part / pixels)[None], (rayleigh_part / pixels)[None])


def solution(mesh):
    placed = (
        P("cuts", "rows", None, None),
        P("cuts", "rows", None),
        P("cuts", None, None, None),
        P("cuts", None, None),
    )
    return jax.shard_map(
        body,
        mesh=mesh,
        in_specs=placed,
        out_specs=(P("cuts", "rows", None, None), P("cuts", "rows", None), P("cuts", "rows", None)),
        check_vma=False,
    )
```

profile of v0, /device:TPU:6, one launch (start us, length us, event | category | flops | bytes accessed | tf_op | source)
XLA Modules:
  0.0 658.2 jit_solution(1508440093911116403)
XLA Ops:
  9.7 4.6 collective-permute-start.1
  14.2 4.1 collective-permute-done
  22.1 5.0 collective-permute-start.3
  27.1 3.2 collective-permute-done.2
  33.4 5.0 collective-permute-start.5
  44.8 5.0 collective-permute-start.7
  54.2 2.5 convolution_bitcast_fusion.5
  57.0 164.4 %all-reduce.14.cloned.1.call-done = f32[128,128]{0,1:T(8,128)} async-done(((f32[128,128]{0,1:T(8,128)}), f32[128,128]{0,1:T(8,128)}) %all-reduce.14.cloned.1.call-update) | async-done | bytes 65552 | tf_op jit(solution)/shard_map/psum | solution.py:66
  223.3 11.7 %cholesky.44 = f32[128,128]{1,0:T(8,128)S(1)} custom-call(f32[128,128]{1,0:T(8,128)S(1)} %fusion.98), custom_call_target="Cholesky" | custom-call | tf_op jit(solution)/shard_map/jit(cholesky)/cholesky | solution.py:67
  236.3 9.8 %custom-call.6 = f32[1,128,128]{1,2,0:T(8,128)S(1)} custom-call(f32[1,128,128]{2,1,0:T(8,128)S(1)} %fusion.89), custom_call_target="InvertDiagBlocksLowerTriangular" | custom-call | tf_op jit(solution)/shard_map/triangular_solve/custom-call.0 | solution.py:68
  248.9 4.6 collective-permute-start.9
  259.2 5.0 collective-permute-start.11
  264.2 2.4 collective-permute-done.10
  270.3 5.0 collective-permute-start.13
  275.3 2.8 collective-permute-done.12
  282.4 5.3 collective-permute-start.15
  291.9 2.5 convolution_bitcast_fusion.3
  294.5 157.7 %all-reduce.16.cloned.1.call-done = f32[128,128]{0,1:T(8,128)} async-done(((f32[128,128]{0,1:T(8,128)}), f32[128,128]{0,1:T(8,128)}) %all-reduce.16.cloned.1.call-update) | async-done | bytes 65552 | tf_op jit(solution)/shard_map/psum | solution.py:66
  454.0 11.7 %cholesky.55 = f32[128,128]{1,0:T(8,128)S(1)} custom-call(f32[128,128]{1,0:T(8,128)S(1)} %fusion.94), custom_call_target="Cholesky" | custom-call | tf_op jit(solution)/shard_map/jit(cholesky)/cholesky | solution.py:67
  467.1 9.8 %custom-call.7 = f32[1,128,128]{1,2,0:T(8,128)S(1)} custom-call(f32[1,128,128]{2,1,0:T(8,128)S(1)} %fusion.90), custom_call_target="InvertDiagBlocksLowerTriangular" | custom-call | tf_op jit(solution)/shard_map/triangular_solve/custom-call.0 | solution.py:68
  482.2 5.3 collective-permute-start.18
  490.7 4.0 convolution_bitcast_fusion
  494.7 2.5 convolution_bitcast_fusion.1
  497.2 153.3 %all-reduce.18.cloned.1.call-done = (f32[128,128]{1,0:T(8,128)}, f32[128,128]{1,0:T(8,128)}) async-done(((f32[128,128]{1,0:T(8,128)}, f32[128,128]{1,0:T(8,128)}), (f32[128,128]{1,0:T(8,128)}, f32[128,128]{1,0:T(8,128)})) %all-reduce.18.cloned.1.call-update) | async-done | bytes 131088 | tf_op jit(solution)/shard_map/psum | solution.py:82
  (78 shorter events, 56.9 us)
Async XLA Ops:
  7.2 214.3 %all-reduce.14.cloned.1.call-start = ((), (), s32[]{:S(2)}) async-start(), calls=%async_computation | async-start | bytes 131072 | tf_op jit(solution)/shard_map/psum | solution.py:66
  8.4 9.9 %collective-permute-start = (f32[1,512,128]{2,1,0:T(8,128)S(1)}, f32[1,512,128]{2,1,0:T(8,128)S(1)}, u32[]{:S(2)}, u32[]{:S(2)}) collective-permute-start(f32[1,512,128]{2,1,0:T(8,128)S(1)} %get-tuple-element.23), channel_id=1, source_target_pairs={{1,0},{2,1},{3,2},{4,3},{5,4},{6,5},{7,6},{8,7},{9,8},{10,9},{11,1... | collective-permute-start | bytes 786440 | tf_op jit(solution)/shard_map/ppermute | solution.py:18
  9.7 9.8 %collective-permute-start.1 = (f32[1,512,128]{2,1,0:T(8,128)S(1)}, f32[1,512,128]{2,1,0:T(8,128)S(1)}, u32[]{:S(2)}, u32[]{:S(2)}) collective-permute-start(f32[1,512,128]{2,1,0:T(8,128)S(1)} %get-tuple-element.24), channel_id=1, source_target_pairs={{0,1},{1,2},{2,3},{3,4},{4,5},{5,6},{6,7},{7,8},{8,9},{9,10},{10,1... | collective-permute-start | bytes 786440 | tf_op jit(solution)/shard_map/ppermute | solution.py:15
  20.8 9.5 %collective-permute-start.2 = (f32[1,512,128]{2,1,0:T(8,128)S(1)}, f32[1,512,128]{2,1,0:T(8,128)S(1)}, u32[]{:S(2)}, u32[]{:S(2)}) collective-permute-start(f32[1,512,128]{2,1,0:T(8,128)S(1)} %get-tuple-element.21), channel_id=1, source_target_pairs={{1,0},{2,1},{3,2},{4,3},{5,4},{6,5},{7,6},{8,7},{9,8},{10,9},{11,1... | collective-permute-start | bytes 786440 | tf_op jit(solution)/shard_map/ppermute | solution.py:18
  22.1 9.4 %collective-permute-start.3 = (f32[1,512,128]{2,1,0:T(8,128)S(1)}, f32[1,512,128]{2,1,0:T(8,128)S(1)}, u32[]{:S(2)}, u32[]{:S(2)}) collective-permute-start(f32[1,512,128]{2,1,0:T(8,128)S(1)} %get-tuple-element.22), channel_id=1, source_target_pairs={{0,1},{1,2},{2,3},{3,4},{4,5},{5,6},{6,7},{7,8},{8,9},{9,10},{10,1... | collective-permute-start | bytes 786440 | tf_op jit(solution)/shard_map/ppermute | solution.py:15
  32.1 8.7 %collective-permute-start.4 = (f32[1,512,128]{2,1,0:T(8,128)S(1)}, f32[1,512,128]{2,1,0:T(8,128)S(1)}, u32[]{:S(2)}, u32[]{:S(2)}) collective-permute-start(f32[1,512,128]{2,1,0:T(8,128)S(1)} %get-tuple-element.19), channel_id=1, source_target_pairs={{1,0},{2,1},{3,2},{4,3},{5,4},{6,5},{7,6},{8,7},{9,8},{10,9},{11,1... | collective-permute-start | bytes 786440 | tf_op jit(solution)/shard_map/ppermute | solution.py:18
  33.4 8.9 %collective-permute-start.5 = (f32[1,512,128]{2,1,0:T(8,128)S(1)}, f32[1,512,128]{2,1,0:T(8,128)S(1)}, u32[]{:S(2)}, u32[]{:S(2)}) collective-permute-start(f32[1,512,128]{2,1,0:T(8,128)S(1)} %get-tuple-element.20), channel_id=1, source_target_pairs={{0,1},{1,2},{2,3},{3,4},{4,5},{5,6},{6,7},{7,8},{8,9},{9,10},{10,1... | collective-permute-start | bytes 786440 | tf_op jit(solution)/shard_map/ppermute | solution.py:15
  43.5 8.7 %collective-permute-start.6 = (f32[1,512,128]{2,1,0:T(8,128)S(1)}, f32[1,512,128]{2,1,0:T(8,128)S(1)}, u32[]{:S(2)}, u32[]{:S(2)}) collective-permute-start(f32[1,512,128]{2,1,0:T(8,128)S(1)} %get-tuple-element.17), channel_id=1, source_target_pairs={{1,0},{2,1},{3,2},{4,3},{5,4},{6,5},{7,6},{8,7},{9,8},{10,9},{11,1... | collective-permute-start | bytes 786440 | tf_op jit(solution)/shard_map/ppermute | solution.py:18
  44.8 8.9 %collective-permute-start.7 = (f32[1,512,128]{2,1,0:T(8,128)S(1)}, f32[1,512,128]{2,1,0:T(8,128)S(1)}, u32[]{:S(2)}, u32[]{:S(2)}) collective-permute-start(f32[1,512,128]{2,1,0:T(8,128)S(1)} %get-tuple-element.18), channel_id=1, source_target_pairs={{0,1},{1,2},{2,3},{3,4},{4,5},{5,6},{6,7},{7,8},{8,9},{9,10},{10,1... | collective-permute-start | bytes 786440 | tf_op jit(solution)/shard_map/ppermute | solution.py:15
  54.2 191.9 %copy-start.3 = (f32[1,2,128,128]{3,2,1,0:T(8,128)S(1)}, f32[1,2,128,128]{3,2,1,0:T(8,128)}, u32[]{:S(2)}) copy-start(f32[1,2,128,128]{3,2,1,0:T(8,128)} %param.9) | copy-start | bytes 393220
  56.8 395.5 %all-reduce.16.cloned.1.call-start = ((), (), s32[]{:S(2)}) async-start(), calls=%async_computation.1 | async-start | bytes 131072 | tf_op jit(solution)/shard_map/psum | solution.py:66
  247.6 8.3 %collective-permute-start.8 = (f32[1,512,128]{2,1,0:T(8,128)S(1)}, f32[1,512,128]{2,1,0:T(8,128)S(1)}, u32[]{:S(2)}, u32[]{:S(2)}) collective-permute-start(f32[1,512,128]{2,1,0:T(8,128)S(1)} %get-tuple-element.15), channel_id=1, source_target_pairs={{1,0},{2,1},{3,2},{4,3},{5,4},{6,5},{7,6},{8,7},{9,8},{10,9},{11,1... | collective-permute-start | bytes 786440 | tf_op jit(solution)/shard_map/ppermute | solution.py:18
  248.9 8.4 %collective-permute-start.9 = (f32[1,512,128]{2,1,0:T(8,128)S(1)}, f32[1,512,128]{2,1,0:T(8,128)S(1)}, u32[]{:S(2)}, u32[]{:S(2)}) collective-permute-start(f32[1,512,128]{2,1,0:T(8,128)S(1)} %get-tuple-element.16), channel_id=1, source_target_pairs={{0,1},{1,2},{2,3},{3,4},{4,5},{5,6},{6,7},{7,8},{8,9},{9,10},{10,1... | collective-permute-start | bytes 786440 | tf_op jit(solution)/shard_map/ppermute | solution.py:15
  257.9 8.7 %collective-permute-start.10 = (f32[1,512,128]{2,1,0:T(8,128)S(1)}, f32[1,512,128]{2,1,0:T(8,128)S(1)}, u32[]{:S(2)}, u32[]{:S(2)}) collective-permute-start(f32[1,512,128]{2,1,0:T(8,128)S(1)} %get-tuple-element.13), channel_id=1, source_target_pairs={{1,0},{2,1},{3,2},{4,3},{5,4},{6,5},{7,6},{8,7},{9,8},{10,9},{11,1... | collective-permute-start | bytes 786440 | tf_op jit(solution)/shard_map/ppermute | solution.py:18
  259.2 9.2 %collective-permute-start.11 = (f32[1,512,128]{2,1,0:T(8,128)S(1)}, f32[1,512,128]{2,1,0:T(8,128)S(1)}, u32[]{:S(2)}, u32[]{:S(2)}) collective-permute-start(f32[1,512,128]{2,1,0:T(8,128)S(1)} %get-tuple-element.14), channel_id=1, source_target_pairs={{0,1},{1,2},{2,3},{3,4},{4,5},{5,6},{6,7},{7,8},{8,9},{9,10},{10,1... | collective-permute-start | bytes 786440 | tf_op jit(solution)/shard_map/ppermute | solution.py:15
  269.0 9.1 %collective-permute-start.12 = (f32[1,512,128]{2,1,0:T(8,128)S(1)}, f32[1,512,128]{2,1,0:T(8,128)S(1)}, u32[]{:S(2)}, u32[]{:S(2)}) collective-permute-start(f32[1,512,128]{2,1,0:T(8,128)S(1)} %get-tuple-element.11), channel_id=1, source_target_pairs={{1,0},{2,1},{3,2},{4,3},{5,4},{6,5},{7,6},{8,7},{9,8},{10,9},{11,1... | collective-permute-start | bytes 786440 | tf_op jit(solution)/shard_map/ppermute | solution.py:18
  270.3 9.5 %collective-permute-start.13 = (f32[1,512,128]{2,1,0:T(8,128)S(1)}, f32[1,512,128]{2,1,0:T(8,128)S(1)}, u32[]{:S(2)}, u32[]{:S(2)}) collective-permute-start(f32[1,512,128]{2,1,0:T(8,128)S(1)} %get-tuple-element.12), channel_id=1, source_target_pairs={{0,1},{1,2},{2,3},{3,4},{4,5},{5,6},{6,7},{7,8},{8,9},{9,10},{10,1... | collective-permute-start | bytes 786440 | tf_op jit(solution)/shard_map/ppermute | solution.py:15
  281.1 8.8 %collective-permute-start.14 = (f32[1,512,128]{2,1,0:T(8,128)S(1)}, f32[1,512,128]{2,1,0:T(8,128)S(1)}, u32[]{:S(2)}, u32[]{:S(2)}) collective-permute-start(f32[1,512,128]{2,1,0:T(8,128)S(1)} %get-tuple-element.9), channel_id=1, source_target_pairs={{1,0},{2,1},{3,2},{4,3},{5,4},{6,5},{7,6},{8,7},{9,8},{10,9},{11,1... | collective-permute-start | bytes 786440 | tf_op jit(solution)/shard_map/ppermute | solution.py:18
  282.4 9.0 %collective-permute-start.15 = (f32[1,512,128]{2,1,0:T(8,128)S(1)}, f32[1,512,128]{2,1,0:T(8,128)S(1)}, u32[]{:S(2)}, u32[]{:S(2)}) collective-permute-start(f32[1,512,128]{2,1,0:T(8,128)S(1)} %get-tuple-element.10), channel_id=1, source_target_pairs={{0,1},{1,2},{2,3},{3,4},{4,5},{5,6},{6,7},{7,8},{8,9},{9,10},{10,1... | collective-permute-start | bytes 786440 | tf_op jit(solution)/shard_map/ppermute | solution.py:15
  294.5 356.0 %all-reduce.18.cloned.1.call-start = ((), (), s32[]{:S(2)}) async-start(), calls=%async_computation.2 | async-start | bytes 262144 | tf_op jit(solution)/shard_map/psum | solution.py:82
  478.3 16.4 %copy-start.1 = (f32[4,512,128]{2,1,0:T(8,128)}, f32[4,512,128]{2,1,0:T(8,128)S(1)}, u32[]{:S(2)}) copy-start(f32[4,512,128]{2,1,0:T(8,128)S(1)} %fusion.118) | copy-start | bytes 3145732
  478.3 16.4 %collective-permute-start.16 = (f32[4,512,128]{2,1,0:T(8,128)S(1)}, f32[4,512,128]{2,1,0:T(8,128)S(1)}, u32[]{:S(2)}, u32[]{:S(2)}) collective-permute-start(f32[4,512,128]{2,1,0:T(8,128)S(1)} %fusion.118), channel_id=1, source_target_pairs={{0,64},{64,128},{128,192},{192,256},{256,320},{320,384},{384,448},... | collective-permute-start | bytes 3145736 | tf_op jit(solution)/shard_map/ppermute | solution.py:26
  480.9 8.6 %collective-permute-start.17 = (f32[1,512,128]{2,1,0:T(8,128)}, f32[1,512,128]{2,1,0:T(8,128)}, u32[]{:S(2)}, u32[]{:S(2)}) collective-permute-start(f32[1,512,128]{2,1,0:T(8,128)} %get-tuple-element.7), channel_id=1, source_target_pairs={{1,0},{2,1},{3,2},{4,3},{5,4},{6,5},{7,6},{8,7},{9,8},{10,9},{11,1... | collective-permute-start | bytes 786440 | tf_op jit(solution)/shard_map/ppermute | solution.py:18
  482.2 8.4 %collective-permute-start.18 = (f32[1,512,128]{2,1,0:T(8,128)S(1)}, f32[1,512,128]{2,1,0:T(8,128)}, u32[]{:S(2)}, u32[]{:S(2)}) collective-permute-start(f32[1,512,128]{2,1,0:T(8,128)S(1)} %get-tuple-element.8), channel_id=1, source_target_pairs={{0,1},{1,2},{2,3},{3,4},{4,5},{5,6},{6,7},{7,8},{8,9},{9,10},{10,1... | collective-permute-start | bytes 786440 | tf_op jit(solution)/shard_map/ppermute | solution.py:15
  (3 other events, 25.8 us)
Sparse Core Ops, SparseCore 0:
  56.9 164.5 all-reduce.13
  294.6 157.5 all-reduce.15
  497.3 153.0 all-reduce.17
where the time goes:
time: 659 us; the launch traced here: 658 us
  waiting for transfers between devices  512 us (78%)
  starting transfers between devices  58.7 us (9%)
  other arithmetic  56.7 us (9%)
  matrix products  14.2 us (2%)
  between operations  14.2 us (2%)
    psum x2, waiting for transfers between devices, body(): gram_sum = lax.psum(inner_modes(current, current), 'rows') / pixels  322 us
    psum x1, waiting for transfers between devices, body(): lax.psum((coupling_term, rayleigh_term), 'rows')  153 us
    ppermute x9, starting transfers between devices, padded_2(): lax.ppermute(lax.slice_in_dim(block, block.shape[dim] - width, None, axis...  44.9 us
    another operation x6, other arithmetic, body(): factor_low = jnp.linalg.cholesky(gram_sum)  24.8 us
    ppermute x9, waiting for transfers between devices, padded_2(): lax.ppermute(lax.slice_in_dim(block, 0, width, axis=dim), axis, backward)  23.8 us
    another operation x4, other arithmetic, body(): lax.linalg.triangular_solve(factor_low, turnings[sweep], left_side=True,...  20.9 us
  transfers between devices with their start and end apart: 22, of which 21 were waited for; matrix products, arithmetic and copies ran while one was open for 1% of the time, Pallas kernels for 0%

commit v1 on v0

v1 whole, which is shorter than its diff:
```python
import functools
import math

import jax
import jax.numpy as jnp
from jax import lax
from jax.experimental import pallas as pl
from jax.experimental.pallas import tpu as pltpu
from jax.sharding import PartitionSpec as P

DEGREE = 4
ITERS = 2
PAD = 8
MESH = pl.DeviceIdType.MESH
HIGH = lax.Precision.HIGHEST


def tdot(a, b):
    return lax.dot_general(
        a, b, (((0,), (0,)), ((), ())), precision=HIGH, preferred_element_type=jnp.float32
    )


def filter_kernel(
    v_hbm, con_hbm, f1_hbm, mats,
    e0, ya, yb, yc, e1, za, zb, zc, f1, coef, con, ctile, earlier, edge, part, land1, land2, tot,
    con_send, con_recv, h1_send, h1_recv, h2_send, h2_recv, e_send, e_recv, x_send, x_recv,
    r_send, r_recv, local,
    *, tiles, peers, slices, cuts1,
):
    rows, cols, nm = v_hbm.shape
    me = lax.axis_index("rows")
    cut = lax.axis_index("cuts")
    up = lax.rem(me + tiles - 1, tiles)
    down = lax.rem(me + 1, tiles)
    my = lax.rem(me, peers)
    mz = me // peers
    nxt = lax.rem(cut + 1, slices)
    prv = lax.rem(cut + slices - 1, slices)
    count = len(cuts1) - 1
    share = nm // peers

    def y_peer(d):
        return mz * peers + lax.rem(my + d, peers)

    def z_peer(d):
        return lax.rem(mz + d, peers) * peers + my

    barrier = pltpu.get_barrier_semaphore()
    for row in [up, down] + [y_peer(d) for d in range(1, peers)] + [z_peer(d) for d in range(1, peers)]:
        pl.semaphore_signal(barrier, inc=1, device_id={"rows": row}, device_id_type=MESH)
    for c in (nxt, prv):
        pl.semaphore_signal(barrier, inc=1, device_id={"cuts": c}, device_id_type=MESH)
    own_v = pltpu.make_async_copy(
        v_hbm, e0.at[pl.ds(rows, rows), pl.ds(PAD, cols), :], local.at[0]
    )
    own_v.start()
    own_c = pltpu.make_async_copy(con_hbm, con.at[1], local.at[1])
    own_c.start()
    pl.semaphore_wait(barrier, 2 * peers + 2)

    con_copies = []
    for side, (peer, slot) in enumerate(((up, 2), (down, 0))):
        cp = pltpu.make_async_remote_copy(
            src_ref=con_hbm, dst_ref=con.at[slot], send_sem=con_send.at[side],
            recv_sem=con_recv.at[side], device_id={"rows": peer}, device_id_type=MESH,
        )
        cp.start()
        con_copies.append(cp)

    def halo(src, dst, send, recv, index, a, b, from_hbm):
        copies = []
        for side, (peer, slot) in enumerate(((up, 2 * rows), (down, 0))):
            source = (
                src.at[:, pl.ds(a, b - a), :] if from_hbm
                else src.at[pl.ds(rows, rows), pl.ds(PAD + a, b - a), :]
            )
            cp = pltpu.make_async_remote_copy(
                src_ref=source, dst_ref=dst.at[pl.ds(slot, rows), pl.ds(PAD + a, b - a), :],
                send_sem=send.at[side, index], recv_sem=recv.at[side, index],
                device_id={"rows": peer}, device_id_type=MESH,
            )
            cp.start()
            copies.append(cp)
        return copies

    first = [
        halo(v_hbm, e0, h1_send, h1_recv, c, cuts1[c], cuts1[c + 1], True) for c in range(count)
    ]

    for ref in (e0, ya, yb, yc, e1, za, zb, zc):
        zero = jnp.zeros((ref.shape[0], PAD, nm), jnp.float32)
        ref[:, pl.ds(0, PAD), :] = zero
        ref[:, pl.ds(PAD + cols, PAD), :] = zero
    f1[:, pl.ds(cols, PAD), :] = jnp.zeros((rows, PAD, nm), jnp.float32)

    own_c.wait()
    for cp in con_copies:
        cp.wait()
    has_up = jnp.where(me > 0, 1.0, 0.0).astype(jnp.float32)
    has_down = jnp.where(me < tiles - 1, 1.0, 0.0).astype(jnp.float32)
    ctile[...] = jnp.zeros_like(ctile)
    for slot, scale in enumerate((has_up, jnp.float32(1.0), has_down)):
        ctile[pl.ds(rows * slot, rows), :] = (1.6 * con[slot] - 0.4) * scale
    for q in range(0, cols, nm):
        flipped = ctile[:, pl.ds(q, nm)].T
        for row in range(3 * rows):
            coef[row, pl.ds(q, nm), :] = jnp.broadcast_to(flipped[:, row : row + 1], (nm, nm))

    def near(i, lo):
        return jnp.where(i < -lo, 0.4 * has_up, jnp.where(i >= rows - lo, 0.4 * has_down, 0.4))

    def stage(dst, dst_off, src, src_off, prev, prev_off, dpad, lo, hi, a, b):
        if b <= a:
            return

        def one(i, _):
            at = pl.ds(PAD + a, b - a)
            s = i + (lo + src_off)
            center = src[s, at, :]
            around = (
                src[s - 1, at, :] + src[s + 1, at, :]
                + src[s, pl.ds(PAD + a - 1, b - a), :] + src[s, pl.ds(PAD + a + 1, b - a), :]
            )
            value = coef[i + (lo + rows), pl.ds(a, b - a), :] * center + near(i, lo) * around
            if prev is None:
                value = 0.5 * value
            else:
                value = value - prev[i + (lo + prev_off), at, :]
            dst[i + (lo + dst_off), pl.ds(dpad + a, b - a), :] = value
            return 0

        lax.fori_loop(0, hi - lo, one, 0)

    def sweep_block(arrays, last, last_off, last_pad, bounds):
        e, y1, y2, y3 = arrays
        (a1, b1), (a2, b2), (a3, b3), (a4, b4) = bounds
        stage(y1, 3, e, rows, None, 0, PAD, -3, rows + 3, a1, b1)
        stage(y2, 2, y1, 3, e, rows, PAD, -2, rows + 2, a2, b2)
        stage(y3, 1, y2, 2, y1, 3, PAD, -1, rows + 1, a3, b3)
        stage(last, last_off, y3, 1, y2, 2, last_pad, 0, rows, a4, b4)

    def bounds_of(edges):
        result = []
        before = [0] * DEGREE
        for c, edge_at in enumerate(edges):
            after = [
                cols if c == len(edges) - 1 else max(0, edge_at - 8 * k) for k in range(1, DEGREE + 1)
            ]
            result.append(list(zip(before, after)))
            before = after
        return result

    def blank(ref, a, b):
        @pl.when(me == 0)
        def _():
            ref[pl.ds(0, rows), pl.ds(PAD + a, b - a), :] = jnp.zeros((rows, b - a, nm), jnp.float32)

        @pl.when(me == tiles - 1)
        def _():
            ref[pl.ds(2 * rows, rows), pl.ds(PAD + a, b - a), :] = jnp.zeros(
                (rows, b - a, nm), jnp.float32
            )

    own_v.wait()
    bounds1 = bounds_of(cuts1[1:])
    second = []
    part[...] = jnp.zeros_like(part)
    for c in range(count):
        for cp in first[c]:
            cp.wait_recv()
        blank(e0, cuts1[c], cuts1[c + 1])
        sweep_block((e0, ya, yb, yc), e1, rows, PAD, bounds1[c])
        a, b = bounds1[c][-1]
        second.append(halo(e1, e1, h2_send, h2_recv, c, a, b, False))
        block = e1[pl.ds(rows, rows), pl.ds(PAD + a, b - a), :].reshape(rows * (b - a), nm)
        part[0] += tdot(block, block)

    bounds2 = bounds_of([b[-1][1] for b in bounds1])
    moved = []
    for c in range(count):
        for cp in second[c]:
            cp.wait_recv()
        blank(e1, *bounds1[c][-1])
        sweep_block((e1, za, zb, zc), f1, 0, 0, bounds2[c])
        a, b = bounds2[c][-1]
        if b > a:
            cp = pltpu.make_async_remote_copy(
                src_ref=f1.at[:, pl.ds(a, b - a), :], dst_ref=earlier.at[:, pl.ds(a, b - a), :],
                send_sem=x_send.at[c], recv_sem=x_recv.at[c],
                device_id={"cuts": nxt}, device_id_type=MESH,
            )
            cp.start()
            moved.append((cp, a, b))
            block = f1[:, pl.ds(a, b - a), :].reshape(rows * (b - a), nm)
            part[1] += tdot(block, block)
    out_f1 = pltpu.make_async_copy(f1.at[:, pl.ds(0, cols), :], f1_hbm, local.at[2])
    out_f1.start()

    half = cols // 2
    lower = pltpu.make_async_remote_copy(
        src_ref=f1.at[0, pl.ds(0, half), :], dst_ref=edge.at[0],
        send_sem=e_send.at[0], recv_sem=e_recv.at[0], device_id={"rows": up}, device_id_type=MESH,
    )
    upper = pltpu.make_async_remote_copy(
        src_ref=f1.at[rows - 1, pl.ds(half, half), :], dst_ref=edge.at[1],
        send_sem=e_send.at[1], recv_sem=e_recv.at[1], device_id={"rows": down}, device_id_type=MESH,
    )
    lower.start()
    upper.start()

    for cp, a, b in moved:
        cp.wait_recv()

        @pl.when(cut == 0)
        def _():
            earlier[:, pl.ds(a, b - a), :] = e0[pl.ds(rows, rows), pl.ds(PAD + a, b - a), :]

        part[3] += tdot(
            earlier[:, pl.ds(a, b - a), :].reshape(rows * (b - a), nm),
            f1[:, pl.ds(a, b - a), :].reshape(rows * (b - a), nm),
        )
    lower.wait_recv()
    upper.wait_recv()
    for row in range(rows):
        for q in range(0, cols, half):
            at = pl.ds(q, half)
            center = f1[row, at, :]
            g = 0.25 * coef[row + rows, at, :] * center + 0.2 * f1[row, pl.ds(q + 1, half), :]
            if row < rows - 1:
                g = g + 0.2 * f1[row + 1, at, :]
            if row == rows - 1 and q == 0:
                g = g + (0.2 * has_down) * edge[0]
            if row == 0 and q > 0:
                g = g + (0.2 * has_up) * edge[1]
            part[2] += tdot(center, g)

    waits = []
    for d in range(1, peers):
        to = lax.rem(my + d, peers)
        cp = pltpu.make_async_remote_copy(
            src_ref=part.at[:, pl.ds(to * share, share), :], dst_ref=land1.at[my],
            send_sem=r_send.at[0, d], recv_sem=r_recv.at[0, d],
            device_id={"rows": y_peer(d)}, device_id_type=MESH,
        )
        cp.start()
        waits.append(cp)
    land1[my] = part[:, pl.ds(my * share, share), :]
    for cp in waits:
        cp.wait()
    total = land1[0]
    for d in range(1, peers):
        total = total + land1[d]
    land2[mz] = total
    waits = []
    for d in range(1, peers):
        cp = pltpu.make_async_remote_copy(
            src_ref=land2.at[mz], dst_ref=land2.at[mz],
            send_sem=r_send.at[1, d], recv_sem=r_recv.at[1, d],
            device_id={"rows": z_peer(d)}, device_id_type=MESH,
        )
        cp.start()
        waits.append(cp)
    for cp in waits:
        cp.wait()
    total = land2[0]
    for d in range(1, peers):
        total = total + land2[d]
    tot[:, pl.ds(my * share, share), :] = total
    waits = []
    for d in range(1, peers):
        cp = pltpu.make_async_remote_copy(
            src_ref=tot.at[:, pl.ds(my * share, share), :],
            dst_ref=tot.at[:, pl.ds(my * share, share), :],
            send_sem=r_send.at[2, d], recv_sem=r_recv.at[2, d],
            device_id={"rows": y_peer(d)}, device_id_type=MESH,
        )
        cp.start()
        waits.append(cp)
    for cp in waits:
        cp.wait()
    mats[...] = tot[...]

    for copies in first + second:
        for cp in copies:
            cp.wait_send()
    for cp, _, _ in moved:
        cp.wait_send()
    lower.wait_send()
    upper.wait_send()
    out_f1.wait()


def run_filter(v, con):
    rows, cols, nm = v.shape
    tiles = lax.axis_size("rows")
    slices = lax.axis_size("cuts")
    peers = math.isqrt(tiles)
    width = cols // 8
    cuts1 = tuple(range(0, cols + 1, width))
    count = len(cuts1) - 1
    wide = cols + 2 * PAD
    f32 = jnp.float32
    vm = lambda *shape: pltpu.VMEM(shape, f32)
    dma = lambda *shape: pltpu.SemaphoreType.DMA(shape)
    share = nm // peers
    return pl.pallas_call(
        functools.partial(filter_kernel, tiles=tiles, peers=peers, slices=slices, cuts1=cuts1),
        out_shape=(
            jax.ShapeDtypeStruct((rows, cols, nm), f32),
            jax.ShapeDtypeStruct((4, nm, nm), f32),
        ),
        in_specs=[pl.BlockSpec(memory_space=pl.ANY)] * 2,
        out_specs=(pl.BlockSpec(memory_space=pl.ANY), pl.BlockSpec(memory_space=pltpu.VMEM)),
        scratch_shapes=[
            vm(12, wide, nm), vm(10, wide, nm), vm(8, wide, nm), vm(6, wide, nm),
            vm(12, wide, nm), vm(10, wide, nm), vm(8, wide, nm), vm(6, wide, nm),
            vm(rows, cols + PAD, nm), vm(12, cols, nm), vm(3, rows, cols), vm(nm, cols),
            vm(rows, cols, nm), vm(2, cols // 2, nm), vm(4, nm, nm),
            vm(peers, 4, share, nm), vm(peers, 4, share, nm), vm(4, nm, nm),
            dma(2), dma(2), dma(2, count), dma(2, count), dma(2, count), dma(2, count),
            dma(2), dma(2), dma(count), dma(count), dma(3, peers), dma(3, peers), dma(3),
        ],
        compiler_params=pltpu.CompilerParams(
            collective_id=0, has_side_effects=True, vmem_limit_bytes=48 * 1024 * 1024
        ),
        cost_estimate=pl.CostEstimate(flops=10**9, bytes_accessed=4 * 2**20, transcendentals=0),
        name="filtered_products",
    )(v, con)


def mix(gram, turning, order):
    nm = gram.shape[0]
    low = jnp.linalg.cholesky(gram)
    mixing = lax.linalg.triangular_solve(low, turning, left_side=True, lower=True, transpose_a=True)
    picker = (order[None, :] == jnp.arange(nm, dtype=jnp.int32)[:, None]).astype(jnp.float32)
    return jnp.dot(mixing, picker, precision=HIGH)


def body(start_modes, contrast, rotations, ordering):
    rows, cols, nm = start_modes.shape[1:]
    tiles = lax.axis_size("rows")
    slices = lax.axis_size("cuts")
    pixels = rows * tiles * cols
    f1, mats = run_filter(start_modes[0], contrast[0])
    dot = functools.partial(jnp.dot, precision=HIGH)
    mats = mats / pixels
    m0 = mix(mats[0], rotations[0, 0], ordering[0, 0])
    m1 = mix(dot(m0.T, dot(mats[1], m0)), rotations[0, 1], ordering[0, 1])
    m = dot(m0, m1)
    modes = jnp.einsum("rcm,mn->rcn", f1, m, precision=HIGH)
    share = nm // tiles
    at = lax.axis_index("rows") * share
    mine = lax.dynamic_slice_in_dim(m, at, share, 1)
    earlier = lax.ppermute(mine, "cuts", [(i, (i + 1) % slices) for i in range(slices)])
    unit = (at + jnp.arange(share)[None, :] == jnp.arange(nm)[:, None]).astype(jnp.float32)
    earlier = jnp.where(lax.axis_index("cuts") == 0, unit, earlier)
    coupling = dot(dot(earlier.T, mats[3]), m)
    rayleigh = dot(dot(mine.T, mats[2] + mats[2].T), m)
    return modes[None], coupling[None], rayleigh[None]


def solution(mesh):
    placed = (
        P("cuts", "rows", None, None),
        P("cuts", "rows", None),
        P("cuts", None, None, None),
        P("cuts", None, None),
    )
    return jax.shard_map(
        body,
        mesh=mesh,
        in_specs=placed,
        out_specs=(P("cuts", "rows", None, None), P("cuts", "rows", None), P("cuts", "rows", None)),
        check_vma=False,
    )
```

time: 659 us -> 149 us (0.23)
  waiting for transfers between devices: 512 us -> 0.01 us
  Pallas kernels: 0 us -> 91.2 us
  starting transfers between devices: 58.7 us -> 0.02 us
  between operations: 14.2 us -> 0.86 us
  other arithmetic: 56.7 us -> 46 us
  matrix products: 14.2 us -> 5.63 us
    psum x3 -> x0, waiting for transfers between devices: 475 us -> none  [the longest x2 322 us: body(): gram_sum = lax.psum(inner_modes(current, current), 'rows') / pixels]
    pallas_call x0 -> x1, Pallas kernels: none -> 91.2 us  [run_filter(): pl.pallas_call(functools.partial(filter_kernel, tiles=tiles, peers=peers,...]
    ppermute x19 -> x1, starting transfers between devices: 58.4 us -> 0.02 us  [body(): lax.ppermute(mine, 'cuts', [(i, (i + 1) % slices) for i in range(slices)])]
    ppermute x19 -> x1, waiting for transfers between devices: 36.6 us -> 0.01 us  [body(): lax.ppermute(mine, 'cuts', [(i, (i + 1) % slices) for i in range(slices)])]
    dot_general x8 -> x10, matrix products: 13.8 us -> 5.22 us  [the longest x1 1.96 us: body(): modes = jnp.einsum('rcm,mn->rcn', f1, m, precision=HIGH)]
  transfers between devices with their start and end apart: 22 -> 1, of which waited for: 21 -> 0; matrix products, arithmetic and copies ran while one was open for 1% -> 2% of each run, Pallas kernels for 0% -> 0%
where the time goes in v1:
time: 149 us; the launch traced here: 146 us
  Pallas kernels  91.2 us (61%)
  other arithmetic  46 us (31%)
  matrix products  5.63 us (4%)
  local copies, waits for them, and re-layouts  2.34 us (2%)
    pallas_call x1, Pallas kernels, run_filter(): pl.pallas_call(functools.partial(filter_kernel, tiles=tiles, peers=peers,...  91.2 us
    another operation x6, other arithmetic, mix(): low = jnp.linalg.cholesky(gram)  25 us
    another operation x4, other arithmetic, mix(): lax.linalg.triangular_solve(low, turning, left_side=True, lower=True, tra...  20.9 us
  transfers between devices with their start and end apart: 1, of which 0 were waited for; matrix products, arithmetic and copies ran while one was open for 2% of the time, Pallas kernels for 0%

profile of v1, /device:TPU:6, one launch (start us, length us, event | category | flops | bytes accessed | tf_op | source)
XLA Modules:
  0.0 146.0 jit_solution(15564883436414309983)
XLA Ops:
  0.6 1.2 copy-done
  1.9 0.7 copy-done.1
  2.6 91.2 %filtered_products.1 = (f32[4,512,128]{2,1,0:T(8,128)S(1)}, f32[4,128,128]{2,1,0:T(8,128)S(1)}) custom-call(f32[4,512,128]{2,1,0:T(8,128)S(1)} %bitcast.69, f32[4,512]{1,0:T(4,128)S(1)} %bitcast.70), custom_call_target="tpu_custom_call" | custom-call | flops 1000000000 | bytes 4194304 | tf_op jit(solution)/shard_map/filtered_products/pallas_call | solution.py:307
  93.8 0.1 copy.7
  94.1 11.7 %cholesky.44 = f32[128,128]{1,0:T(8,128)S(1)} custom-call(f32[128,128]{1,0:T(8,128)S(1)} %fusion.4), custom_call_target="Cholesky" | custom-call | tf_op jit(solution)/shard_map/jit(cholesky)/cholesky | solution.py:334
  105.9 0.6 compare_reduce_fusion.1
  106.5 0.7 fusion
  107.2 9.8 %custom-call.6 = f32[1,128,128]{1,2,0:T(8,128)S(1)} custom-call(f32[1,128,128]{2,1,0:T(8,128)S(1)} %fusion), custom_call_target="InvertDiagBlocksLowerTriangular" | custom-call | tf_op jit(solution)/shard_map/triangular_solve/custom-call.0 | solution.py:335
  117.0 0.2 fusion.11
  117.2 0.2 fusion.16
  117.4 0.3 fusion.3
  117.7 0.3 fusion.25
  118.1 11.9 %cholesky.55 = f32[128,128]{1,0:T(8,128)S(1)} custom-call(f32[128,128]{1,0:T(8,128)S(1)} %fusion.10), custom_call_target="Cholesky" | custom-call | tf_op jit(solution)/shard_map/jit(cholesky)/cholesky | solution.py:334
  130.1 0.6 compare_reduce_fusion
  130.7 0.7 fusion.1
  131.4 9.8 %custom-call.7 = f32[1,128,128]{1,2,0:T(8,128)S(1)} custom-call(f32[1,128,128]{2,1,0:T(8,128)S(1)} %fusion.1), custom_call_target="InvertDiagBlocksLowerTriangular" | custom-call | tf_op jit(solution)/shard_map/triangular_solve/custom-call.0 | solution.py:335
  141.2 0.2 fusion.7
  141.4 0.2 fusion.17
  141.6 0.3 fusion.26
  142.0 0.2 fusion.5
  142.2 0.8 convolution_bitcast_fusion.1
  143.0 2.0 %convolution_bitcast_fusion = f32[1,4,512,128]{3,2,1,0:T(8,128)} fusion(f32[4,512,128]{2,1,0:T(8,128)S(1)} %get-tuple-element.7, f32[128,128]{0,1:T(8,128)S(1)} %fusion.26), kind=kOutput, calls=%fused_computation | convolution fusion | flops 402653184 | bytes 2162688 | tf_op jit(solution)/shard_map/rcm,mn->rcn/dot_general | solution.py:351
  145.0 0.2 fusion.2
  145.2 0.8 convolution_bitcast_fusion.2
  (20 shorter events, 0.4 us)
Async XLA Ops:
  0.6 1.2 copy-start
  1.9 0.7 copy-start.1
  94.1 22.9 %copy-start.2 = (f32[1,2,128,128]{3,2,1,0:T(8,128)S(1)}, f32[1,2,128,128]{3,2,1,0:T(8,128)}, u32[]{:S(2)}) copy-start(f32[1,2,128,128]{3,2,1,0:T(8,128)} %param.9) | copy-start | bytes 393220
  107.2 9.8 %copy-start.3 = (s32[1,2,128]{2,1,0:T(2,128)S(1)}, s32[1,2,128]{2,1,0:T(2,128)}, u32[]{:S(2)}) copy-start(s32[1,2,128]{2,1,0:T(2,128)} %param.10) | copy-start | bytes 3076
  141.9 3.1 %collective-permute-start = (f32[128,2]{0,1:T(2,128)S(1)}, f32[128,2]{0,1:T(2,128)S(1)}, u32[]{:S(2)}, u32[]{:S(2)}) collective-permute-start(f32[128,2]{0,1:T(2,128)S(1)} %constant_dynamic-slice_fusion), channel_id=1, source_target_pairs={{0,64},{64,128},{128,192},{192,256},{256,320},{320,384},{384,448},... | collective-permute-start | bytes 3080 | tf_op jit(solution)/shard_map/ppermute | solution.py:355

commit v2 on v1

--- a/solution.py
+++ b/solution.py
@@ -21,11 +21,55 @@
     )
 
 
-def filter_kernel(
-    v_hbm, con_hbm, f1_hbm, mats,
-    e0, ya, yb, yc, e1, za, zb, zc, f1, coef, con, ctile, earlier, edge, part, land1, land2, tot,
+def dot(a, b):
+    return jnp.dot(a, b, precision=HIGH, preferred_element_type=jnp.float32)
+
+
+def ones_where(condition):
+    return jnp.where(condition, 1.0, 0.0).astype(jnp.float32)
+
+
+def eliminate(gram, inverse, first, last):
+    nm = gram.shape[0]
+    row = lax.broadcasted_iota(jnp.int32, (8, nm), 0)
+    for panel in range(first, last):
+        o = 8 * panel
+        rest = nm - o - 8
+        sh, eh = gram[pl.ds(o, 8), :], inverse[pl.ds(o, 8), :]
+        ch = [jnp.broadcast_to(sh[:, o + k : o + k + 1], (8, nm)) for k in range(8)]
+        if rest:
+            st, et = gram[pl.ds(o + 8, rest), :], inverse[pl.ds(o + 8, rest), :]
+            ct = [jnp.broadcast_to(st[:, o + k : o + k + 1], (rest, nm)) for k in range(8)]
+        pivots = jnp.ones((8, nm), jnp.float32)
+        for j in range(8):
+            pivot = ch[j][j : j + 1, :]
+            scale = 1.0 / pivot
+            pivots = jnp.where(row == j, pivot, pivots)
+            rs, re = sh[j : j + 1, :], eh[j : j + 1, :]
+            rc = [c[j : j + 1, :] for c in ch]
+            mh = jnp.where(row > j, ch[j] * scale, 0.0)
+            for k in range(j + 1, 8):
+                ch[k] = ch[k] - mh * rc[k]
+            sh = sh - mh * rs
+            eh = eh - mh * re
+            if rest:
+                mt = ct[j] * scale
+                for k in range(j + 1, 8):
+                    ct[k] = ct[k] - mt * rc[k]
+                st = st - mt * rs
+                et = et - mt * re
+        inverse[pl.ds(o, 8), :] = eh * lax.rsqrt(pivots)
+        if rest:
+            gram[pl.ds(o + 8, rest), :] = st
+            inverse[pl.ds(o + 8, rest), :] = et
+
+
+def lantern_kernel(
+    v_hbm, con_hbm, rot_hbm, order_hbm, modes_hbm, coupling_out, rayleigh_out,
+    e0, ya, yb, yc, e1, za, zb, zc, f1, coef, con, ctile, earlier, edge, vout,
+    part0, part1, part2, landa, landb, tot0, tot1, tot2, rot, order, gram, inverse, m0, mine, before,
     con_send, con_recv, h1_send, h1_recv, h2_send, h2_recv, e_send, e_recv, x_send, x_recv,
-    r_send, r_recv, local,
+    r_send, r_recv, m_send, m_recv, local,
     *, tiles, peers, slices, cuts1,
 ):
     rows, cols, nm = v_hbm.shape
@@ -57,6 +101,10 @@
     own_v.start()
     own_c = pltpu.make_async_copy(con_hbm, con.at[1], local.at[1])
     own_c.start()
+    own_r = pltpu.make_async_copy(rot_hbm, rot, local.at[2])
+    own_r.start()
+    own_o = pltpu.make_async_copy(order_hbm, order, local.at[3])
+    own_o.start()
     pl.semaphore_wait(barrier, 2 * peers + 2)
 
     con_copies = []
@@ -107,6 +155,14 @@
         for row in range(3 * rows):
             coef[row, pl.ds(q, nm), :] = jnp.broadcast_to(flipped[:, row : row + 1], (nm, nm))
 
+    own_r.wait()
+    own_o.wait()
+    index = lax.broadcasted_iota(jnp.int32, (nm, nm), 0)
+    for t in range(ITERS):
+        picker = ones_where(index == jnp.broadcast_to(order[pl.ds(t, 1), :], (nm, nm)))
+        rot[t] = dot(rot[t], picker)
+    unit = ones_where(index == lax.broadcasted_iota(jnp.int32, (nm, nm), 1))
+
     def near(i, lo):
         return jnp.where(i < -lo, 0.4 * has_up, jnp.where(i >= rows - lo, 0.4 * has_down, 0.4))
 
@@ -162,10 +218,62 @@
                 (rows, b - a, nm), jnp.float32
             )
 
+    def summing(which, part, total):
+        count = part.shape[0]
+        lo = sum((1, 1, 2)[:which])
+        land1 = landa.at[:, pl.ds(lo, count)]
+        land2 = landb.at[:, pl.ds(lo, count)]
+        ours = pl.ds(my * share, share)
+        started = []
+
+        def send(step, d, src, dst, row):
+            cp = pltpu.make_async_remote_copy(
+                src_ref=src, dst_ref=dst, send_sem=r_send.at[which, step, d],
+                recv_sem=r_recv.at[which, step, d], device_id={"rows": row}, device_id_type=MESH,
+            )
+            cp.start()
+            started.append(cp)
+
+        def finish():
+            for cp in started:
+                cp.wait()
+            started.clear()
+
+        def added(land):
+            value = land[0]
+            for d in range(1, peers):
+                value = value + land[d]
+            return value
+
+        def spread():
+            for d in range(1, peers):
+                to = pl.ds(lax.rem(my + d, peers) * share, share)
+                send(0, d, part.at[:, to, :], land1.at[my], y_peer(d))
+            land1[my] = part[:, ours, :]
+
+        def across():
+            finish()
+            land2[mz] = added(land1)
+            for d in range(1, peers):
+                send(1, d, land2.at[mz], land2.at[mz], z_peer(d))
+
+        def gather():
+            finish()
+            total[:, ours, :] = added(land2) * (1.0 / (rows * tiles * cols))
+            for d in range(1, peers):
+                send(2, d, total.at[:, ours, :], total.at[:, ours, :], y_peer(d))
+
+        return spread, across, gather, finish
+
+    sum0 = summing(0, part0, tot0)
+    sum1 = summing(1, part1, tot1)
+    sum2 = summing(2, part2, tot2)
+
     own_v.wait()
     bounds1 = bounds_of(cuts1[1:])
     second = []
-    part[...] = jnp.zeros_like(part)
+    for ref in (part0, part1, part2):
+        ref[...] = jnp.zeros_like(ref)
     for c in range(count):
         for cp in first[c]:
             cp.wait_recv()
@@ -174,7 +282,38 @@
         a, b = bounds1[c][-1]
         second.append(halo(e1, e1, h2_send, h2_recv, c, a, b, False))
         block = e1[pl.ds(rows, rows), pl.ds(PAD + a, b - a), :].reshape(rows * (b - a), nm)
-        part[0] += tdot(block, block)
+        part0[0] += tdot(block, block)
+    sum0[0]()
+
+    def start_inverse(value):
+        gram[...] = value
+        inverse[...] = unit
+
+    def first_mixing():
+        eliminate(gram, inverse, third * 2, nm // 8)
+        m0[...] = tdot(inverse[...], rot[0])
+
+    third = nm // 24
+    between = {
+        0: sum0[1],
+        1: sum0[2],
+        2: lambda: (sum0[3](), start_inverse(tot0[0]), eliminate(gram, inverse, 0, third)),
+        3: lambda: eliminate(gram, inverse, third, third * 2),
+        4: first_mixing,
+    }
+
+    def correlate(item):
+        cp, a, b = item
+        cp.wait_recv()
+
+        @pl.when(cut == 0)
+        def _():
+            earlier[:, pl.ds(a, b - a), :] = e0[pl.ds(rows, rows), pl.ds(PAD + a, b - a), :]
+
+        part2[1] += tdot(
+            earlier[:, pl.ds(a, b - a), :].reshape(rows * (b - a), nm),
+            f1[:, pl.ds(a, b - a), :].reshape(rows * (b - a), nm),
+        )
 
     bounds2 = bounds_of([b[-1][1] for b in bounds1])
     moved = []
@@ -193,9 +332,12 @@
             cp.start()
             moved.append((cp, a, b))
             block = f1[:, pl.ds(a, b - a), :].reshape(rows * (b - a), nm)
-            part[1] += tdot(block, block)
-    out_f1 = pltpu.make_async_copy(f1.at[:, pl.ds(0, cols), :], f1_hbm, local.at[2])
-    out_f1.start()
+            part1[0] += tdot(block, block)
+        if len(moved) > 2:
+            correlate(moved[len(moved) - 3])
+        if c in between:
+            between[c]()
+    sum1[0]()
 
     half = cols // 2
     lower = pltpu.make_async_remote_copy(
@@ -209,17 +351,9 @@
     lower.start()
     upper.start()
 
-    for cp, a, b in moved:
-        cp.wait_recv()
-
-        @pl.when(cut == 0)
-        def _():
-            earlier[:, pl.ds(a, b - a), :] = e0[pl.ds(rows, rows), pl.ds(PAD + a, b - a), :]
-
-        part[3] += tdot(
-            earlier[:, pl.ds(a, b - a), :].reshape(rows * (b - a), nm),
-            f1[:, pl.ds(a, b - a), :].reshape(rows * (b - a), nm),
-        )
+    for item in moved[-2:]:
+        correlate(item)
+    sum1[1]()
     lower.wait_recv()
     upper.wait_recv()
     for row in range(rows):
@@ -233,53 +367,45 @@
                 g = g + (0.2 * has_down) * edge[0]
             if row == 0 and q > 0:
                 g = g + (0.2 * has_up) * edge[1]
-            part[2] += tdot(center, g)
-
-    waits = []
-    for d in range(1, peers):
-        to = lax.rem(my + d, peers)
-        cp = pltpu.make_async_remote_copy(
-            src_ref=part.at[:, pl.ds(to * share, share), :], dst_ref=land1.at[my],
-            send_sem=r_send.at[0, d], recv_sem=r_recv.at[0, d],
-            device_id={"rows": y_peer(d)}, device_id_type=MESH,
-        )
+            part2[0] += tdot(center, g)
+        if row == rows // 2 - 1:
+            sum1[2]()
+    sum2[0]()
+
+    sum1[3]()
+    start_inverse(tdot(m0[...], dot(tot1[0], m0[...])))
+    eliminate(gram, inverse, 0, third)
+    sum2[1]()
+    eliminate(gram, inverse, third, third * 2)
+    sum2[2]()
+    eliminate(gram, inverse, third * 2, nm // 8)
+    mixing = dot(m0[...], tdot(inverse[...], rot[1]))
+    picked = mine.shape[0]
+    at = me * (nm // tiles)
+    chosen = ones_where(
+        lax.broadcasted_iota(jnp.int32, (picked, nm), 0) + at
+        == lax.broadcasted_iota(jnp.int32, (picked, nm), 1)
+    )
+    mine[...] = lax.dot_general(
+        chosen, mixing, (((1,), (1,)), ((), ())), precision=HIGH, preferred_element_type=jnp.float32
+    )
+    onward = pltpu.make_async_remote_copy(
+        src_ref=mine, dst_ref=before, send_sem=m_send, recv_sem=m_recv,
+        device_id={"cuts": nxt}, device_id_type=MESH,
+    )
+    onward.start()
+    outs = []
+    for row in range(rows):
+        vout[row] = dot(f1[row, pl.ds(0, cols), :], mixing)
+        cp = pltpu.make_async_copy(vout.at[row], modes_hbm.at[row], local.at[4 + row])
         cp.start()
-        waits.append(cp)
-    land1[my] = part[:, pl.ds(my * share, share), :]
-    for cp in waits:
-        cp.wait()
-    total = land1[0]
-    for d in range(1, peers):
-        total = total + land1[d]
-    land2[mz] = total
-    waits = []
-    for d in range(1, peers):
-        cp = pltpu.make_async_remote_copy(
-            src_ref=land2.at[mz], dst_ref=land2.at[mz],
-            send_sem=r_send.at[1, d], recv_sem=r_recv.at[1, d],
-            device_id={"rows": z_peer(d)}, device_id_type=MESH,
-        )
-        cp.start()
-        waits.append(cp)
-    for cp in waits:
-        cp.wait()
-    total = land2[0]
-    for d in range(1, peers):
-        total = total + land2[d]
-    tot[:, pl.ds(my * share, share), :] = total
-    waits = []
-    for d in range(1, peers):
-        cp = pltpu.make_async_remote_copy(
-            src_ref=tot.at[:, pl.ds(my * share, share), :],
-            dst_ref=tot.at[:, pl.ds(my * share, share), :],
-            send_sem=r_send.at[2, d], recv_sem=r_recv.at[2, d],
-            device_id={"rows": y_peer(d)}, device_id_type=MESH,
-        )
-        cp.start()
-        waits.append(cp)
-    for cp in waits:
-        cp.wait()
-    mats[...] = tot[...]
+        outs.append(cp)
+    sum2[3]()
+    both = tot2[0]
+    rayleigh_out[...] = dot(dot(mine[...], both + both.T), mixing)
+    onward.wait()
+    left = jnp.where(cut == 0, chosen, before[...])
+    coupling_out[...] = dot(dot(left, tot2[1]), mixing)
 
     for copies in first + second:
         for cp in copies:
@@ -288,11 +414,12 @@
         cp.wait_send()
     lower.wait_send()
     upper.wait_send()
-    out_f1.wait()
-
-
-def run_filter(v, con):
-    rows, cols, nm = v.shape
+    for cp in outs:
+        cp.wait()
+
+
+def body(start_modes, contrast, rotations, ordering):
+    rows, cols, nm = start_modes.shape[1:]
     tiles = lax.axis_size("rows")
     slices = lax.axis_size("cuts")
     peers = math.isqrt(tiles)
@@ -304,60 +431,39 @@
     vm = lambda *shape: pltpu.VMEM(shape, f32)
     dma = lambda *shape: pltpu.SemaphoreType.DMA(shape)
     share = nm // peers
-    return pl.pallas_call(
-        functools.partial(filter_kernel, tiles=tiles, peers=peers, slices=slices, cuts1=cuts1),
+    kept = nm // tiles
+    picked = max(8, kept)
+    hbm = pl.BlockSpec(memory_space=pltpu.HBM)
+    modes, coupling, rayleigh = pl.pallas_call(
+        functools.partial(lantern_kernel, tiles=tiles, peers=peers, slices=slices, cuts1=cuts1),
         out_shape=(
             jax.ShapeDtypeStruct((rows, cols, nm), f32),
-            jax.ShapeDtypeStruct((4, nm, nm), f32),
+            jax.ShapeDtypeStruct((picked, nm), f32),
+            jax.ShapeDtypeStruct((picked, nm), f32),
         ),
-        in_specs=[pl.BlockSpec(memory_space=pl.ANY)] * 2,
-        out_specs=(pl.BlockSpec(memory_space=pl.ANY), pl.BlockSpec(memory_space=pltpu.VMEM)),
+        in_specs=[hbm] * 4,
+        out_specs=(hbm,) + (pl.BlockSpec(memory_space=pltpu.VMEM),) * 2,
         scratch_shapes=[
             vm(12, wide, nm), vm(10, wide, nm), vm(8, wide, nm), vm(6, wide, nm),
             vm(12, wide, nm), vm(10, wide, nm), vm(8, wide, nm), vm(6, wide, nm),
             vm(rows, cols + PAD, nm), vm(12, cols, nm), vm(3, rows, cols), vm(nm, cols),
-            vm(rows, cols, nm), vm(2, cols // 2, nm), vm(4, nm, nm),
-            vm(peers, 4, share, nm), vm(peers, 4, share, nm), vm(4, nm, nm),
+            vm(rows, cols, nm), vm(2, cols // 2, nm), vm(rows, cols, nm),
+            vm(1, nm, nm), vm(1, nm, nm), vm(2, nm, nm),
+            vm(peers, 4, share, nm), vm(peers, 4, share, nm),
+            vm(1, nm, nm), vm(1, nm, nm), vm(2, nm, nm),
+            vm(ITERS, nm, nm), pltpu.VMEM((ITERS, nm), jnp.int32),
+            vm(nm, nm), vm(nm, nm), vm(nm, nm), vm(picked, nm), vm(picked, nm),
             dma(2), dma(2), dma(2, count), dma(2, count), dma(2, count), dma(2, count),
-            dma(2), dma(2), dma(count), dma(count), dma(3, peers), dma(3, peers), dma(3),
+            dma(2), dma(2), dma(count), dma(count), dma(3, 3, peers), dma(3, 3, peers),
+            pltpu.SemaphoreType.DMA, pltpu.SemaphoreType.DMA, dma(4 + rows),
         ],
         compiler_params=pltpu.CompilerParams(
-            collective_id=0, has_side_effects=True, vmem_limit_bytes=48 * 1024 * 1024
+            collective_id=0, has_side_effects=True, vmem_limit_bytes=56 * 1024 * 1024
         ),
         cost_estimate=pl.CostEstimate(flops=10**9, bytes_accessed=4 * 2**20, transcendentals=0),
-        name="filtered_products",
-    )(v, con)
-
-
-def mix(gram, turning, order):
-    nm = gram.shape[0]
-    low = jnp.linalg.cholesky(gram)
-    mixing = lax.linalg.triangular_solve(low, turning, left_side=True, lower=True, transpose_a=True)
-    picker = (order[None, :] == jnp.arange(nm, dtype=jnp.int32)[:, None]).astype(jnp.float32)
-    return jnp.dot(mixing, picker, precision=HIGH)
-
-
-def body(start_modes, contrast, rotations, ordering):
-    rows, cols, nm = start_modes.shape[1:]
-    tiles = lax.axis_size("rows")
-    slices = lax.axis_size("cuts")
-    pixels = rows * tiles * cols
-    f1, mats = run_filter(start_modes[0], contrast[0])
-    dot = functools.partial(jnp.dot, precision=HIGH)
-    mats = mats / pixels
-    m0 = mix(mats[0], rotations[0, 0], ordering[0, 0])
-    m1 = mix(dot(m0.T, dot(mats[1], m0)), rotations[0, 1], ordering[0, 1])
-    m = dot(m0, m1)
-    modes = jnp.einsum("rcm,mn->rcn", f1, m, precision=HIGH)
-    share = nm // tiles
-    at = lax.axis_index("rows") * share
-    mine = lax.dynamic_slice_in_dim(m, at, share, 1)
-    earlier = lax.ppermute(mine, "cuts", [(i, (i + 1) % slices) for i in range(slices)])
-    unit = (at + jnp.arange(share)[None, :] == jnp.arange(nm)[:, None]).astype(jnp.float32)
-    earlier = jnp.where(lax.axis_index("cuts") == 0, unit, earlier)
-    coupling = dot(dot(earlier.T, mats[3]), m)
-    rayleigh = dot(dot(mine.T, mats[2] + mats[2].T), m)
-    return modes[None], coupling[None], rayleigh[None]
+        name="lantern",
+    )(start_modes[0], contrast[0], rotations[0], ordering[0])
+    return modes[None], coupling[None, :kept], rayleigh[None, :kept]
 
 
 def solution(mesh):

time: 149 us -> 121 us (0.81); the launches traced: 146 us -> 120 us
  other arithmetic: 46 us -> 0 us
  Pallas kernels: 91.2 us -> 116 us
  matrix products: 5.63 us -> 0 us
    another operation x10 -> x0, other arithmetic: 45.9 us -> none  [the longest x6 25 us: mix(): low = jnp.linalg.cholesky(gram)]
    pallas_call x1, Pallas kernels: 91.2 us -> 116 us  [body(): pl.pallas_call(functools.partial(lantern_kernel, tiles=tiles, peers=peers...]
    dot_general x10 -> x0, matrix products: 5.22 us -> none  [the longest x1 1.96 us: body(): modes = jnp.einsum('rcm,mn->rcn', f1, m, precision=HIGH)]
  transfers between devices with their start and end apart: 1 -> 0, of which waited for: 0 -> 0; matrix products, arithmetic and copies ran while one was open for 2% -> 0% of each run, Pallas kernels for 0% -> 0%
where the time goes in v2:
time: 121 us; the launch traced here: 120 us
  Pallas kernels  116 us (96%)
  local copies, waits for them, and re-layouts  3.51 us (3%)
    pallas_call x1, Pallas kernels, body(): pl.pallas_call(functools.partial(lantern_kernel, tiles=tiles, peers=peers...  116 us

profile of v2, /device:TPU:6, one launch (start us, length us, event | category | flops | bytes accessed | tf_op | source)
XLA Modules:
  0.0 120.3 jit_solution(16487156609839088471)
XLA Ops:
  0.6 116.2 %lantern.1 = (f32[4,512,128]{2,1,0:T(8,128)}, f32[8,128]{1,0:T(8,128)}, f32[8,128]{1,0:T(8,128)}) custom-call(f32[4,512,128]{2,1,0:T(8,128)} %bitcast.10, f32[4,512]{1,0:T(4,128)} %bitcast.12, f32[2,128,128]{2,1,0:T(8,128)} %bitcast.11, s32[2,128]{1,0:T(2,128)} %bitcast.13), custom_call_target="tpu_custom_call" | custom-call | flops 1000000000 | bytes 4194304 | tf_op jit(solution)/shard_map/lantern/pallas_call | solution.py:437
  116.8 1.2 %slice_bitcast_fusion = (f32[1,2,128]{2,1,0:T(2,128)}, f32[1,2,128]{2,1,0:T(2,128)}) fusion(f32[8,128]{1,0:T(8,128)} %get-tuple-element.8, f32[8,128]{1,0:T(8,128)} %get-tuple-element.7), kind=kLoop, calls=%fused_computation | loop fusion | bytes 4096 | tf_op jit(solution)/shard_map/broadcast_in_dim | solution.py:466
  118.1 2.3 %copy.8 = f32[1,4,512,128]{3,2,1,0:T(8,128)} copy(f32[1,4,512,128]{3,2,1,0:T(8,128)} %bitcast.9) | data formatting | bytes 2097152

commit v3 on v2

--- a/solution.py
+++ b/solution.py
@@ -11,6 +11,7 @@
 DEGREE = 4
 ITERS = 2
 PAD = 8
+AHEAD = 2
 MESH = pl.DeviceIdType.MESH
 HIGH = lax.Precision.HIGHEST
 
@@ -65,8 +66,8 @@
 
 
 def lantern_kernel(
-    v_hbm, con_hbm, rot_hbm, order_hbm, modes_hbm, coupling_out, rayleigh_out,
-    e0, ya, yb, yc, e1, za, zb, zc, f1, coef, con, ctile, earlier, edge, vout,
+    v_hbm, con_hbm, rot_hbm, order_hbm, modes_out, coupling_out, rayleigh_out,
+    e0, ya, yb, yc, e1, za, zb, zc, f1, coef, con, ctile, earlier, edge,
     part0, part1, part2, landa, landb, tot0, tot1, tot2, rot, order, gram, inverse, m0, mine, before,
     con_send, con_recv, h1_send, h1_recv, h2_send, h2_recv, e_send, e_recv, x_send, x_recv,
     r_send, r_recv, m_send, m_recv, local,
@@ -280,7 +281,8 @@
         blank(e0, cuts1[c], cuts1[c + 1])
         sweep_block((e0, ya, yb, yc), e1, rows, PAD, bounds1[c])
         a, b = bounds1[c][-1]
-        second.append(halo(e1, e1, h2_send, h2_recv, c, a, b, False))
+        if c < AHEAD:
+            second.append(halo(e1, e1, h2_send, h2_recv, c, a, b, False))
         block = e1[pl.ds(rows, rows), pl.ds(PAD + a, b - a), :].reshape(rows * (b - a), nm)
         part0[0] += tdot(block, block)
     sum0[0]()
@@ -290,17 +292,13 @@
         inverse[...] = unit
 
     def first_mixing():
-        eliminate(gram, inverse, third * 2, nm // 8)
+        sum0[3]()
+        start_inverse(tot0[0])
+        eliminate(gram, inverse, 0, nm // 8)
         m0[...] = tdot(inverse[...], rot[0])
 
     third = nm // 24
-    between = {
-        0: sum0[1],
-        1: sum0[2],
-        2: lambda: (sum0[3](), start_inverse(tot0[0]), eliminate(gram, inverse, 0, third)),
-        3: lambda: eliminate(gram, inverse, third, third * 2),
-        4: first_mixing,
-    }
+    between = {3: sum0[1], 6: sum0[2]}
 
     def correlate(item):
         cp, a, b = item
@@ -320,6 +318,8 @@
     for c in range(count):
         for cp in second[c]:
             cp.wait_recv()
+        if c + AHEAD < count:
+            second.append(halo(e1, e1, h2_send, h2_recv, c + AHEAD, *bounds1[c + AHEAD][-1], False))
         blank(e1, *bounds1[c][-1])
         sweep_block((e1, za, zb, zc), f1, 0, 0, bounds2[c])
         a, b = bounds2[c][-1]
@@ -353,6 +353,7 @@
 
     for item in moved[-2:]:
         correlate(item)
+    first_mixing()
     sum1[1]()
     lower.wait_recv()
     upper.wait_recv()
@@ -368,8 +369,7 @@
             if row == 0 and q > 0:
                 g = g + (0.2 * has_up) * edge[1]
             part2[0] += tdot(center, g)
-        if row == rows // 2 - 1:
-            sum1[2]()
+    sum1[2]()
     sum2[0]()
 
     sum1[3]()
@@ -394,18 +394,14 @@
         device_id={"cuts": nxt}, device_id_type=MESH,
     )
     onward.start()
-    outs = []
     for row in range(rows):
-        vout[row] = dot(f1[row, pl.ds(0, cols), :], mixing)
-        cp = pltpu.make_async_copy(vout.at[row], modes_hbm.at[row], local.at[4 + row])
-        cp.start()
-        outs.append(cp)
+        modes_out[row] = dot(f1[row, pl.ds(0, cols), :], mixing)
     sum2[3]()
     both = tot2[0]
-    rayleigh_out[...] = dot(dot(mine[...], both + both.T), mixing)
+    rayleigh_out[...] = dot(dot(mine[...], both + both.T), mixing)[: rayleigh_out.shape[0]]
     onward.wait()
     left = jnp.where(cut == 0, chosen, before[...])
-    coupling_out[...] = dot(dot(left, tot2[1]), mixing)
+    coupling_out[...] = dot(dot(left, tot2[1]), mixing)[: coupling_out.shape[0]]
 
     for copies in first + second:
         for cp in copies:
@@ -414,8 +410,6 @@
         cp.wait_send()
     lower.wait_send()
     upper.wait_send()
-    for cp in outs:
-        cp.wait()
 
 
 def body(start_modes, contrast, rotations, ordering):
@@ -438,16 +432,16 @@
         functools.partial(lantern_kernel, tiles=tiles, peers=peers, slices=slices, cuts1=cuts1),
         out_shape=(
             jax.ShapeDtypeStruct((rows, cols, nm), f32),
-            jax.ShapeDtypeStruct((picked, nm), f32),
-            jax.ShapeDtypeStruct((picked, nm), f32),
+            jax.ShapeDtypeStruct((kept, nm), f32),
+            jax.ShapeDtypeStruct((kept, nm), f32),
         ),
         in_specs=[hbm] * 4,
-        out_specs=(hbm,) + (pl.BlockSpec(memory_space=pltpu.VMEM),) * 2,
+        out_specs=(pl.BlockSpec(memory_space=pltpu.VMEM),) * 3,
         scratch_shapes=[
             vm(12, wide, nm), vm(10, wide, nm), vm(8, wide, nm), vm(6, wide, nm),
             vm(12, wide, nm), vm(10, wide, nm), vm(8, wide, nm), vm(6, wide, nm),
             vm(rows, cols + PAD, nm), vm(12, cols, nm), vm(3, rows, cols), vm(nm, cols),
-            vm(rows, cols, nm), vm(2, cols // 2, nm), vm(rows, cols, nm),
+            vm(rows, cols, nm), vm(2, cols // 2, nm),
             vm(1, nm, nm), vm(1, nm, nm), vm(2, nm, nm),
             vm(peers, 4, share, nm), vm(peers, 4, share, nm),
             vm(1, nm, nm), vm(1, nm, nm), vm(2, nm, nm),
@@ -455,15 +449,15 @@
             vm(nm, nm), vm(nm, nm), vm(nm, nm), vm(picked, nm), vm(picked, nm),
             dma(2), dma(2), dma(2, count), dma(2, count), dma(2, count), dma(2, count),
             dma(2), dma(2), dma(count), dma(count), dma(3, 3, peers), dma(3, 3, peers),
-            pltpu.SemaphoreType.DMA, pltpu.SemaphoreType.DMA, dma(4 + rows),
+            pltpu.SemaphoreType.DMA, pltpu.SemaphoreType.DMA, dma(4),
         ],
         compiler_params=pltpu.CompilerParams(
-            collective_id=0, has_side_effects=True, vmem_limit_bytes=56 * 1024 * 1024
+            collective_id=0, has_side_effects=True, vmem_limit_bytes=40 * 1024 * 1024
         ),
         cost_estimate=pl.CostEstimate(flops=10**9, bytes_accessed=4 * 2**20, transcendentals=0),
         name="lantern",
     )(start_modes[0], contrast[0], rotations[0], ordering[0])
-    return modes[None], coupling[None, :kept], rayleigh[None, :kept]
+    return modes[None], coupling[None], rayleigh[None]
 
 
 def solution(mesh):

time: 121 us -> 112 us (0.926)
  Pallas kernels: 116 us -> 105 us
  local copies, waits for them, and re-layouts: 3.51 us -> 5.59 us
    pallas_call x1, Pallas kernels: 116 us -> 105 us  [body(): pl.pallas_call(functools.partial(lantern_kernel, tiles=tiles, peers=peers...]
    unnamed x1 -> x11, local copies, waits for them, and re-layouts: 2.26 us -> 5.59 us
    broadcast_in_dim x1 -> x0, local copies, waits for them, and re-layouts: 1.25 us -> none  [body(): return (modes[None], coupling[None, :kept], rayleigh[None, :kept])]
where the time goes in v3:
time: 112 us; the launch traced here: 111 us
  Pallas kernels  105 us (94%)
  local copies, waits for them, and re-layouts  5.59 us (5%)
    pallas_call x1, Pallas kernels, body(): pl.pallas_call(functools.partial(lantern_kernel, tiles=tiles, peers=peers...  105 us
    unnamed x11, local copies, waits for them, and re-layouts  5.59 us

profile of v3, /device:TPU:6, one launch (start us, length us, event | category | flops | bytes accessed | tf_op | source)
XLA Modules:
  0.0 110.8 jit_solution(10362234481873300134)
XLA Ops:
  0.6 0.0 copy-start.3
  0.6 0.7 copy-done.3
  1.3 0.0 copy-start
  1.3 1.2 %copy-done = f32[1,4,512,128]{3,2,1,0:T(8,128)S(1)} copy-done((f32[1,4,512,128]{3,2,1,0:T(8,128)S(1)}, f32[1,4,512,128]{3,2,1,0:T(8,128)}, u32[]{:S(2)}) %copy-start) | copy-done | bytes 1048600
  2.5 0.0 copy-start.1
  2.5 0.9 copy-done.1
  3.4 0.0 copy-start.2
  3.4 0.7 copy-done.2
  4.1 104.5 %lantern.1 = (f32[4,512,128]{2,1,0:T(8,128)S(1)}, f32[2,128]{1,0:T(2,128)S(1)}, f32[2,128]{1,0:T(2,128)S(1)}) custom-call(f32[4,512,128]{2,1,0:T(8,128)S(1)} %bitcast.10, f32[4,512]{1,0:T(4,128)S(1)} %bitcast.12, f32[2,128,128]{2,1,0:T(8,128)S(1)} %bitcast.11, s32[2,128]{1,0:T(2,128)S(1)} %bitcast.13), custom_call_target="tpu_custom_call" | custom-call | flops 1000000000 | bytes 4194304 | tf_op jit(solution)/shard_map/lantern/pallas_call | solution.py:431
  108.7 1.0 copy.10
  109.7 0.6 copy.11
  110.2 0.6 copy.12
Async XLA Ops:
  0.6 0.7 copy-start.3
  1.3 1.2 %copy-start = (f32[1,4,512,128]{3,2,1,0:T(8,128)S(1)}, f32[1,4,512,128]{3,2,1,0:T(8,128)}, u32[]{:S(2)}) copy-start(f32[1,4,512,128]{3,2,1,0:T(8,128)} %param.4) | copy-start | bytes 3145732
  2.5 0.9 copy-start.1
  3.4 0.7 copy-start.2

commit v4 on v3

--- a/solution.py
+++ b/solution.py
@@ -11,7 +11,6 @@
 DEGREE = 4
 ITERS = 2
 PAD = 8
-AHEAD = 2
 MESH = pl.DeviceIdType.MESH
 HIGH = lax.Precision.HIGHEST
 
@@ -68,7 +67,7 @@
 def lantern_kernel(
     v_hbm, con_hbm, rot_hbm, order_hbm, modes_out, coupling_out, rayleigh_out,
     e0, ya, yb, yc, e1, za, zb, zc, f1, coef, con, ctile, earlier, edge,
-    part0, part1, part2, landa, landb, tot0, tot1, tot2, rot, order, gram, inverse, m0, mine, before,
+    part1, part2, landa, landb, tot1, tot2, rot, order, gram, inverse, m0, mine, before,
     con_send, con_recv, h1_send, h1_recv, h2_send, h2_recv, e_send, e_recv, x_send, x_recv,
     r_send, r_recv, m_send, m_recv, local,
     *, tiles, peers, slices, cuts1,
@@ -221,7 +220,7 @@
 
     def summing(which, part, total):
         count = part.shape[0]
-        lo = sum((1, 1, 2)[:which])
+        lo = (0, 0, 2)[which]
         land1 = landa.at[:, pl.ds(lo, count)]
         land2 = landb.at[:, pl.ds(lo, count)]
         ours = pl.ds(my * share, share)
@@ -266,14 +265,13 @@
 
         return spread, across, gather, finish
 
-    sum0 = summing(0, part0, tot0)
     sum1 = summing(1, part1, tot1)
     sum2 = summing(2, part2, tot2)
 
     own_v.wait()
     bounds1 = bounds_of(cuts1[1:])
     second = []
-    for ref in (part0, part1, part2):
+    for ref in (part1, part2):
         ref[...] = jnp.zeros_like(ref)
     for c in range(count):
         for cp in first[c]:
@@ -281,24 +279,20 @@
         blank(e0, cuts1[c], cuts1[c + 1])
         sweep_block((e0, ya, yb, yc), e1, rows, PAD, bounds1[c])
         a, b = bounds1[c][-1]
-        if c < AHEAD:
-            second.append(halo(e1, e1, h2_send, h2_recv, c, a, b, False))
+        second.append(halo(e1, e1, h2_send, h2_recv, c, a, b, False))
         block = e1[pl.ds(rows, rows), pl.ds(PAD + a, b - a), :].reshape(rows * (b - a), nm)
-        part0[0] += tdot(block, block)
-    sum0[0]()
+        part1[1] += tdot(block, block)
 
     def start_inverse(value):
         gram[...] = value
         inverse[...] = unit
 
     def first_mixing():
-        sum0[3]()
-        start_inverse(tot0[0])
+        start_inverse(tot1[1])
         eliminate(gram, inverse, 0, nm // 8)
         m0[...] = tdot(inverse[...], rot[0])
 
     third = nm // 24
-    between = {3: sum0[1], 6: sum0[2]}
 
     def correlate(item):
         cp, a, b = item
@@ -318,8 +312,6 @@
     for c in range(count):
         for cp in second[c]:
             cp.wait_recv()
-        if c + AHEAD < count:
-            second.append(halo(e1, e1, h2_send, h2_recv, c + AHEAD, *bounds1[c + AHEAD][-1], False))
         blank(e1, *bounds1[c][-1])
         sweep_block((e1, za, zb, zc), f1, 0, 0, bounds2[c])
         a, b = bounds2[c][-1]
@@ -335,8 +327,6 @@
             part1[0] += tdot(block, block)
         if len(moved) > 2:
             correlate(moved[len(moved) - 3])
-        if c in between:
-            between[c]()
     sum1[0]()
 
     half = cols // 2
@@ -353,7 +343,6 @@
 
     for item in moved[-2:]:
         correlate(item)
-    first_mixing()
     sum1[1]()
     lower.wait_recv()
     upper.wait_recv()
@@ -373,12 +362,12 @@
     sum2[0]()
 
     sum1[3]()
+    sum2[1]()
+    first_mixing()
     start_inverse(tdot(m0[...], dot(tot1[0], m0[...])))
     eliminate(gram, inverse, 0, third)
-    sum2[1]()
-    eliminate(gram, inverse, third, third * 2)
     sum2[2]()
-    eliminate(gram, inverse, third * 2, nm // 8)
+    eliminate(gram, inverse, third, nm // 8)
     mixing = dot(m0[...], tdot(inverse[...], rot[1]))
     picked = mine.shape[0]
     at = me * (nm // tiles)
@@ -442,9 +431,9 @@
             vm(12, wide, nm), vm(10, wide, nm), vm(8, wide, nm), vm(6, wide, nm),
             vm(rows, cols + PAD, nm), vm(12, cols, nm), vm(3, rows, cols), vm(nm, cols),
             vm(rows, cols, nm), vm(2, cols // 2, nm),
-            vm(1, nm, nm), vm(1, nm, nm), vm(2, nm, nm),
+            vm(2, nm, nm), vm(2, nm, nm),
             vm(peers, 4, share, nm), vm(peers, 4, share, nm),
-            vm(1, nm, nm), vm(1, nm, nm), vm(2, nm, nm),
+            vm(2, nm, nm), vm(2, nm, nm),
             vm(ITERS, nm, nm), pltpu.VMEM((ITERS, nm), jnp.int32),
             vm(nm, nm), vm(nm, nm), vm(nm, nm), vm(picked, nm), vm(picked, nm),
             dma(2), dma(2), dma(2, count), dma(2, count), dma(2, count), dma(2, count),
@@ -452,7 +441,7 @@
             pltpu.SemaphoreType.DMA, pltpu.SemaphoreType.DMA, dma(4),
         ],
         compiler_params=pltpu.CompilerParams(
-            collective_id=0, has_side_effects=True, vmem_limit_bytes=40 * 1024 * 1024
+            collective_id=0, has_side_effects=True, vmem_limit_bytes=56 * 1024 * 1024
         ),
         cost_estimate=pl.CostEstimate(flops=10**9, bytes_accessed=4 * 2**20, transcendentals=0),
         name="lantern",

time: 112 us -> 103 us (0.920)
  Pallas kernels: 105 us -> 98.5 us
  local copies, waits for them, and re-layouts: 5.59 us -> 3.49 us
    pallas_call x1, Pallas kernels: 105 us -> 98.5 us  [body(): pl.pallas_call(functools.partial(lantern_kernel, tiles=tiles, peers=peers...]
    unnamed x11 -> x7, local copies, waits for them, and re-layouts: 5.59 us -> 3.49 us
where the time goes in v4:
time: 103 us
  Pallas kernels  98.5 us (96%)
  local copies, waits for them, and re-layouts  3.49 us (3%)
    pallas_call x1, Pallas kernels, body(): pl.pallas_call(functools.partial(lantern_kernel, tiles=tiles, peers=peers...  98.5 us
    unnamed x7, local copies, waits for them, and re-layouts  3.49 us

profile of v4, /device:TPU:6, one launch (start us, length us, event | category | flops | bytes accessed | tf_op | source)
XLA Modules:
  0.0 102.6 jit_solution(9907686985513351811)
XLA Ops:
  0.6 98.5 %lantern.1 = (f32[4,512,128]{2,1,0:T(8,128)}, f32[2,128]{1,0:T(2,128)}, f32[2,128]{1,0:T(2,128)}) custom-call(f32[4,512,128]{2,1,0:T(8,128)} %bitcast.10, f32[4,512]{1,0:T(4,128)} %bitcast.12, f32[2,128,128]{2,1,0:T(8,128)} %bitcast.11, s32[2,128]{1,0:T(2,128)} %bitcast.13), custom_call_target="tpu_custom_call" | custom-call | flops 1000000000 | bytes 4194304 | tf_op jit(solution)/shard_map/lantern/pallas_call | solution.py:420
  99.1 0.0 copy-start.1
  99.2 2.3 %copy.10 = f32[1,4,512,128]{3,2,1,0:T(8,128)} copy(f32[1,4,512,128]{3,2,1,0:T(8,128)} %bitcast.7) | data formatting | bytes 2097152
  101.4 0.0 copy-done.1
  101.4 0.0 copy-start
  101.4 0.6 copy.11
  102.0 0.1 copy-done
  102.1 0.6 copy.12
Async XLA Ops:
  99.1 2.3 %copy-start.1 = (f32[2,128]{1,0:T(2,128)S(1)}, f32[2,128]{1,0:T(2,128)}, u32[]{:S(2)}) copy-start(f32[2,128]{1,0:T(2,128)} %get-tuple-element.7) | copy-start | bytes 3076
  101.4 0.7 copy-start

commit v5 on v4

--- a/solution.py
+++ b/solution.py
@@ -67,7 +67,7 @@
 def lantern_kernel(
     v_hbm, con_hbm, rot_hbm, order_hbm, modes_out, coupling_out, rayleigh_out,
     e0, ya, yb, yc, e1, za, zb, zc, f1, coef, con, ctile, earlier, edge,
-    part1, part2, landa, landb, tot1, tot2, rot, order, gram, inverse, m0, mine, before,
+    part0, part1, part2, landa, landb, tot0, tot1, tot2, rot, order, gram, inverse, m0, mine, before,
     con_send, con_recv, h1_send, h1_recv, h2_send, h2_recv, e_send, e_recv, x_send, x_recv,
     r_send, r_recv, m_send, m_recv, local,
     *, tiles, peers, slices, cuts1,
@@ -220,7 +220,7 @@
 
     def summing(which, part, total):
         count = part.shape[0]
-        lo = (0, 0, 2)[which]
+        lo = (0, 1, 2)[which]
         land1 = landa.at[:, pl.ds(lo, count)]
         land2 = landb.at[:, pl.ds(lo, count)]
         ours = pl.ds(my * share, share)
@@ -265,13 +265,14 @@
 
         return spread, across, gather, finish
 
+    sum0 = summing(0, part0, tot0)
     sum1 = summing(1, part1, tot1)
     sum2 = summing(2, part2, tot2)
 
     own_v.wait()
     bounds1 = bounds_of(cuts1[1:])
     second = []
-    for ref in (part1, part2):
+    for ref in (part0, part1, part2):
         ref[...] = jnp.zeros_like(ref)
     for c in range(count):
         for cp in first[c]:
@@ -281,14 +282,15 @@
         a, b = bounds1[c][-1]
         second.append(halo(e1, e1, h2_send, h2_recv, c, a, b, False))
         block = e1[pl.ds(rows, rows), pl.ds(PAD + a, b - a), :].reshape(rows * (b - a), nm)
-        part1[1] += tdot(block, block)
+        part0[0] += tdot(block, block)
+    sum0[0]()
 
     def start_inverse(value):
         gram[...] = value
         inverse[...] = unit
 
     def first_mixing():
-        start_inverse(tot1[1])
+        start_inverse(tot0[0])
         eliminate(gram, inverse, 0, nm // 8)
         m0[...] = tdot(inverse[...], rot[0])
 
@@ -340,10 +342,12 @@
     )
     lower.start()
     upper.start()
+    sum0[1]()
 
     for item in moved[-2:]:
         correlate(item)
     sum1[1]()
+    sum0[2]()
     lower.wait_recv()
     upper.wait_recv()
     for row in range(rows):
@@ -358,12 +362,13 @@
             if row == 0 and q > 0:
                 g = g + (0.2 * has_up) * edge[1]
             part2[0] += tdot(center, g)
+    sum2[0]()
     sum1[2]()
-    sum2[0]()
+    sum0[3]()
+    first_mixing()
+    sum2[1]()
 
     sum1[3]()
-    sum2[1]()
-    first_mixing()
     start_inverse(tdot(m0[...], dot(tot1[0], m0[...])))
     eliminate(gram, inverse, 0, third)
     sum2[2]()
@@ -431,9 +436,9 @@
             vm(12, wide, nm), vm(10, wide, nm), vm(8, wide, nm), vm(6, wide, nm),
             vm(rows, cols + PAD, nm), vm(12, cols, nm), vm(3, rows, cols), vm(nm, cols),
             vm(rows, cols, nm), vm(2, cols // 2, nm),
-            vm(2, nm, nm), vm(2, nm, nm),
+            vm(1, nm, nm), vm(1, nm, nm), vm(2, nm, nm),
             vm(peers, 4, share, nm), vm(peers, 4, share, nm),
-            vm(2, nm, nm), vm(2, nm, nm),
+            vm(1, nm, nm), vm(1, nm, nm), vm(2, nm, nm),
             vm(ITERS, nm, nm), pltpu.VMEM((ITERS, nm), jnp.int32),
             vm(nm, nm), vm(nm, nm), vm(nm, nm), vm(picked, nm), vm(picked, nm),
             dma(2), dma(2), dma(2, count), dma(2, count), dma(2, count), dma(2, count),

time: 103 us -> 102 us (level)
  no operation moved by 1% of the time
where the time goes in v5:
time: 102 us
  Pallas kernels  97.5 us (96%)
  local copies, waits for them, and re-layouts  3.49 us (3%)
    pallas_call x1, Pallas kernels, body(): pl.pallas_call(functools.partial(lantern_kernel, tiles=tiles, peers=peers...  97.5 us
    unnamed x7, local copies, waits for them, and re-layouts  3.49 us

profile of v5, /device:TPU:6, one launch (start us, length us, event | category | flops | bytes accessed | tf_op | source)
XLA Modules:
  0.0 101.6 jit_solution(17125847917026816190)
XLA Ops:
  0.6 97.5 %lantern.1 = (f32[4,512,128]{2,1,0:T(8,128)}, f32[2,128]{1,0:T(2,128)}, f32[2,128]{1,0:T(2,128)}) custom-call(f32[4,512,128]{2,1,0:T(8,128)} %bitcast.10, f32[4,512]{1,0:T(4,128)} %bitcast.12, f32[2,128,128]{2,1,0:T(8,128)} %bitcast.11, s32[2,128]{1,0:T(2,128)} %bitcast.13), custom_call_target="tpu_custom_call" | custom-call | flops 1000000000 | bytes 4194304 | tf_op jit(solution)/shard_map/lantern/pallas_call | solution.py:425
  98.1 0.0 copy-start.1
  98.1 2.3 %copy.10 = f32[1,4,512,128]{3,2,1,0:T(8,128)} copy(f32[1,4,512,128]{3,2,1,0:T(8,128)} %bitcast.7) | data formatting | bytes 2097152
  100.4 0.0 copy-done.1
  100.4 0.0 copy-start
  100.4 0.6 copy.11
  101.0 0.1 copy-done
  101.1 0.6 copy.12
Async XLA Ops:
  98.1 2.3 %copy-start.1 = (f32[2,128]{1,0:T(2,128)S(1)}, f32[2,128]{1,0:T(2,128)}, u32[]{:S(2)}) copy-start(f32[2,128]{1,0:T(2,128)} %get-tuple-element.7) | copy-start | bytes 3076
  100.4 0.7 copy-start
